TPU v7x, 512 devices: a whole 4x4x16 slice. The times are simulated.
512 devices in a mesh: fsdp: 128 (over z, x, core), rep: 4 (over y).
Axes of the slice: x: 4, y: 4, z: 16, core: 2. Of those that a mesh axis runs over, the one named last changes fastest.
Arguments:
- gradients: bfloat16 [4, 512, 48, 3584], P('rep', 'fsdp'), may hold values from -6 to 6
- owner: int32 [336], replicated, may hold values from 0 to 127, as said below
- left_stats: float32 [512, 512, 512], P(('fsdp', 'rep')), may hold values from -0.0625 to 3072, as said below
- right_stats: float32 [512, 512, 512], P(('fsdp', 'rep')), may hold values from -0.0625 to 3072, as said below
Outputs:
- update: bfloat16 [512, 48, 3584], P('fsdp')
Inputs may be any that keep to these rules, and one draw needn't show every extreme that they name: No owner holds more than 4 blocks, and some owner holds exactly 4. `left_stats`: each entry is symmetric and positive definite. `right_stats`: each entry is symmetric and positive definite.
All inputs are finite; a program needn't handle non-finite values.
Results may differ from a plain program's by a relative error of at most 0.014.
Values may be sent and summed in bfloat16 or wider, within the bound.
A program may use at most 64 MiB of HBM per device.

v0:
```python
import jax
import jax.numpy as jnp
from jax import lax
from jax.sharding import PartitionSpec as P

ITERS = 2


def exact_dot(lhs_mat, rhs_mat):
    return jnp.dot(
        lhs_mat, rhs_mat, precision=lax.Precision.HIGHEST, preferred_element_type=jnp.float32
    )


def slot_table(owner, owners, replicas):
    total_blocks = owner.shape[0]
    matches = (owner[:, None] == jnp.arange(owners, dtype=jnp.int32)[None, :]).astype(jnp.int32)
    before = jnp.cumsum(matches, axis=0) - matches
    slot_of = jnp.sum(before * matches, axis=1)
    key_ids = owner * replicas + slot_of
    slot_hits = (
        key_ids[:, None] == jnp.arange(owners * replicas, dtype=jnp.int32)[None, :]
    ).astype(jnp.int32)
    block_ids = jnp.arange(total_blocks, dtype=jnp.int32)
    block_of = jnp.sum(slot_hits * (block_ids - total_blocks)[:, None], axis=0) + total_blocks
    return (block_of, slot_of)


def inverse_fourth_root(matrix):
    extent = matrix.shape[0]
    fro_norm = jnp.sqrt(jnp.sum(matrix * matrix))
    factor = 2.5 / fro_norm
    identity = jnp.eye(extent, dtype=jnp.float32)
    coupled = factor * matrix
    root_mat = identity
    for sweep_index in range(ITERS):
        update_term = (5.0 * identity - coupled) * 0.25
        if sweep_index == 0:
            root_mat = jnp.sqrt(jnp.sqrt(factor)) * update_term
        else:
            root_mat = exact_dot(root_mat, update_term)
        if sweep_index + 1 < ITERS:
            square = exact_dot(update_term, update_term)
            coupled = exact_dot(exact_dot(square, square), coupled)
    return root_mat


def shampoo_block(grad_block, left_stat, right_stat):
    outer_gram = lax.dot_general(
        grad_block, grad_block, (((1,), (1,)), ((), ())), preferred_element_type=jnp.float32
    )
    inner_gram = lax.dot_general(
        grad_block, grad_block, (((0,), (0,)), ((), ())), preferred_element_type=jnp.float32
    )
    left_root = inverse_fourth_root(left_stat + outer_gram)
    right_root = inverse_fourth_root(right_stat + inner_gram)
    dense_grad = grad_block.astype(jnp.float32)
    shaped = exact_dot(exact_dot(left_root, dense_grad), right_root)
    grad_rms = jnp.sqrt(jnp.mean(dense_grad * dense_grad))
    shaped_rms = jnp.sqrt(jnp.mean(shaped * shaped) + 1e-06)
    return (shaped * (grad_rms / shaped_rms)).astype(jnp.bfloat16)


def per_device(gradients, owner, left_stats, right_stats):
    owners = lax.axis_size("fsdp")
    replicas = lax.axis_size("rep")
    rep_rank = lax.axis_index("rep")
    own_rows = gradients[0]
    row_count, row_blocks, col_width = own_rows.shape
    extent = row_count * owners
    blocks = owner.shape[0]
    block_of, slot_of = slot_table(owner, owners, replicas)
    by_slot = block_of.reshape(owners, replicas)
    filler = jnp.zeros((row_count, 1, extent), jnp.bfloat16)
    summed = lax.psum(own_rows.astype(jnp.float32).astype(jnp.bfloat16), "rep").astype(jnp.float32)
    averaged = (summed * (1.0 / replicas)).astype(jnp.bfloat16)
    pieces = jnp.concatenate([averaged.reshape(row_count, blocks, extent), filler], axis=1)
    my_blocks = lax.dynamic_index_in_dim(by_slot, rep_rank, axis=1, keepdims=False)
    outgoing = jnp.take(pieces, my_blocks, axis=1)
    arrived = lax.all_to_all(outgoing, "fsdp", split_axis=1, concat_axis=0, tiled=True)
    grad_block = arrived.reshape(extent, extent)
    update = shampoo_block(grad_block, left_stats[0], right_stats[0])
    returned = lax.all_to_all(
        update.reshape(extent, 1, extent), "fsdp", split_axis=0, concat_axis=1, tiled=True
    )
    collected = lax.all_gather(returned[:, None], "rep", axis=1, tiled=True)
    flattened = collected.reshape(row_count, replicas * owners, extent)
    picked = jnp.take(flattened, slot_of * owners + owner, axis=1)
    return picked.reshape(row_count, row_blocks, col_width)


def solution(mesh):
    placed = (
        P("rep", "fsdp", None, None),
        P(),
        P(("fsdp", "rep"), None, None),
        P(("fsdp", "rep"), None, None),
    )
    return jax.shard_map(
        per_device, mesh=mesh, in_specs=placed, out_specs=P("fsdp", None, None), check_vma=False
    )
```

profile of v0, /device:TPU:1, one launch (start us, length us, event | category | flops | bytes accessed | tf_op | source)
XLA Modules:
  0.0 252.8 jit_solution(9367303074156230483)
XLA Ops:
  8.6 69.2 %all-reduce.4.cloned.1.call-done = bf16[4,48,3584]{2,1,0:T(8,128)(2,1)} async-done(((bf16[4,48,3584]{2,1,0:T(8,128)(2,1)}), bf16[4,48,3584]{2,1,0:T(8,128)(2,1)}) %all-reduce.4.cloned.1.call-update) | async-done | bytes 1376272 | tf_op jit(solution)/shard_map/psum | solution.py:75
  77.8 1.6 multiply_convert_fusion
  79.4 1.5 reshape.56
  80.9 1.1 copy.39
  82.5 1.0 gather_fusion
  83.9 48.2 %all_to_all.30 = bf16[4,128,512]{2,0,1:T(4,128)(2,1)S(1)} all-to-all(bf16[4,128,512]{2,0,1:T(4,128)(2,1)S(1)} %select_bitcast_fusion), channel_id=1, replica_groups=mesh['fsdp'=128,'rep'=4] {'fsdp'}, dimensions={1} | all-to-all | bytes 1048576 | tf_op jit(solution)/shard_map/all_to_all | solution.py:80
  133.4 1.2 multiply_reduce_fusion.3
  135.3 2.0 fusion.7
  137.3 1.8 fusion.49
  139.1 1.9 fusion
  141.1 2.0 fusion.9
  144.3 1.2 multiply_reduce_fusion.2
  146.2 2.0 fusion.3
  148.2 2.1 fusion.51
  150.2 2.8 %fusion.1 = f32[512,512]{1,0:T(8,128)} fusion(f32[512,512]{1,0:T(8,128)S(1)} %fusion.51, f32[512,512]{1,0:T(8,128)S(1)} %get-tuple-element.10, f32[]{:T(128)S(6)} %div.16), kind=kOutput, calls=%fused_computation.11 | convolution fusion | flops 1611923456 | bytes 3145732 | tf_op jit(solution)/shard_map/dot_general | solution.py:10
  154.8 3.2 %fusion.5 = f32[512,512]{1,0:T(8,128)S(1)} fusion(f32[512,512]{1,0:T(8,128)} %fusion.1, f32[512,512]{1,0:T(8,128)S(1)} %get-tuple-element.10, f32[]{:T(128)S(6)} %mul.121, f32[]{:T(128)S(6)} %div.16), kind=kOutput, calls=%fused_computation.18 | convolution fusion | flops 1611923456 | bytes 3145736 | tf_op jit(solution)/shard_map/dot_general | solution.py:10
  158.0 2.6 %multiply_reduce_fusion = (f32[]{:T(128)}, f32[512,512]{1,0:T(8,128)S(1)}) fusion(f32[512,512]{1,0:T(8,128)S(1)} %fusion.50, f32[512,512]{1,0:T(8,128)S(1)} %fusion.5), kind=kOutput, calls=%fused_computation.14 | convolution fusion | flops 1611137024 | bytes 3145732 | tf_op jit(solution)/shard_map/dot_general | solution.py:10
  161.9 1.0 reduce.6
  163.3 39.8 %all_to_all.31 = bf16[128,2,1024]{2,1,0:T(2,128)(2,1)S(1)} all-to-all(bf16[128,2,1024]{2,1,0:T(2,128)(2,1)S(1)} %reshape.85), channel_id=1, replica_groups=mesh['fsdp'=128,'rep'=4] {'fsdp'}, dimensions={0} | all-to-all | bytes 1048576 | tf_op jit(solution)/shard_map/all_to_all | solution.py:83
  203.5 3.2 %reduce.3 = bf16[512,512]{1,0:T(8,128)(2,1)S(1)} reduce(bf16[512,1,512]{2,1,0:T(2,128)(2,1)S(1)} %reshape.86, bf16[]{:T(256)} %constant.81), dimensions={1}, to_apply=%all_to_all.25.reduce_sub_computation | reduce | bytes 1048578 | tf_op jit(solution)/shard_map/all_to_all | solution.py:83
  208.0 31.4 %all-gather.3.cloned.1.call-done = bf16[4,512,1,512]{3,0,2,1:T(4,128)(2,1)} async-done(((bf16[4,128,1,512]{3,0,2,1:T(4,128)(2,1)}), bf16[4,512,1,512]{3,0,2,1:T(4,128)(2,1)}) %all-gather.3.cloned.1.call-update) | async-done | bytes 2097168 | tf_op jit(solution)/shard_map/all_gather | solution.py:86
  239.5 3.5 %gather_fusion.1 = bf16[336,4,512]{2,1,0:T(4,128)(2,1)S(1)} fusion(bf16[4,512,512]{2,0,1:T(4,128)(2,1)} %bitcast.62, s32[1024]{0:T(1024)S(1)} %pad_clamp_fusion), kind=kCustom, calls=%fused_computation.1 | custom fusion | bytes 2753856 | tf_op jit(solution)/shard_map/jit(_take)/gather | solution.py:88
  243.2 1.5 gather.12
  244.7 1.3 broadcast_select_fusion
  (43 shorter events, 9.2 us)
Async XLA Ops:
  6.5 0.8 copy-start.2
  6.5 71.3 %all-reduce.4.cloned.1.call-start = ((), (), s32[]{:S(2)}) async-start(), calls=%async_computation.2 | async-start | bytes 2752512 | tf_op jit(solution)/shard_map/psum | solution.py:75
  7.3 232.2 %all-gather.3.cloned.1.call-start = ((), (), s32[]{:S(2)}) async-start(), calls=%async_computation.3 | async-start | bytes 2621440 | tf_op jit(solution)/shard_map/all_gather | solution.py:86
  132.1 1.2 copy-start
  143.0 1.2 copy-start.1
Sparse Core Ops, SparseCore 0:
  9.7 68.0 all-reduce.3
  207.7 31.6 all-gather.2
where the time goes:
time: 253 us
  waiting for transfers between devices  101 us (40%)
  blocking collectives  88 us (35%)
  matrix products  23.7 us (9%)
  between operations  16.7 us (7%)
  local copies, waits for them, and re-layouts  13.5 us (5%)
  other arithmetic  9.59 us (4%)
    psum x1, waiting for transfers between devices, per_device(): lax.psum(own_rows.astype(jnp.float32).astype(jnp.bfloat16), 'rep')  69.2 us
    all_to_all x1, blocking collectives, per_device(): lax.all_to_all(outgoing, 'fsdp', split_axis=1, concat_axis=0, tiled=True)  48.2 us
    all_to_all x1, blocking collectives, per_device(): lax.all_to_all(update.reshape(extent, 1, extent), 'fsdp', split_axis=0, c...  39.8 us
    all_gather x1, waiting for transfers between devices, per_device(): collected = lax.all_gather(returned[:, None], 'rep', axis=1, tiled=True)  31.4 us
    dot_general x10, matrix products, exact_dot(): jnp.dot(lhs_mat, rhs_mat, precision=lax.Precision.HIGHEST, preferred_elem...  21.3 us
    gather x3, local copies, waits for them, and re-layouts, per_device(): picked = jnp.take(flattened, slot_of * owners + owner, axis=1)  5.24 us
  transfers between devices with their start and end apart: 2, of which 2 were waited for; matrix products, arithmetic and copies ran while one was open for 1% of the time, Pallas kernels for 0%

commit v1 on v0

v1 whole, which is shorter than its diff:
```python
import functools

import jax
import jax.numpy as jnp
import numpy as np
from jax import lax
from jax.experimental import pallas as pl
from jax.experimental.pallas import tpu as pltpu
from jax.sharding import PartitionSpec as P

MESH = pl.DeviceIdType.MESH
PER_Z = 8
PIECES = 4
ORDER_BITS = 10

F32 = jnp.float32
BF16 = jnp.bfloat16


def mm(lhs, rhs):
    return lax.dot_general(lhs, rhs, (((1,), (0,)), ((), ())), preferred_element_type=F32)


def mm_nt(lhs, rhs):
    return lax.dot_general(lhs, rhs, (((1,), (1,)), ((), ())), preferred_element_type=F32)


def mm_tn(lhs, rhs):
    return lax.dot_general(lhs, rhs, (((0,), (0,)), ((), ())), preferred_element_type=F32)


def one_hot(mask):
    return jnp.where(mask, 1.0, 0.0).astype(BF16)


def newton_root(acc):
    factor = 2.5 / jnp.sqrt(jnp.sum(acc * acc))
    m = acc * factor
    mb = m.astype(BF16)
    q = mm(mb, mb) * 0.0625 - 0.625 * m
    t = 1.5625 * m + mm(q.astype(BF16), mb)
    r = 1.25 * q - 0.25 * t
    rest = -0.3125 * m - 0.25 * (1.953125 * t + mm(r.astype(BF16), t.astype(BF16)))
    return factor, rest


def kernel(
    dims,
    grads,
    rank_row,
    rank_col,
    left,
    right,
    out,
    own,
    stats,
    yrecv,
    zsend,
    zrecv,
    psend,
    precv,
    asend,
    arecv,
    bsend,
    brecv,
    vsend,
    to_key,
    to_block,
    to_slot,
    to_z,
    gmat,
    pmat,
    local_sem,
    send_sem,
    y_sem,
    z_sem,
    p_sem,
    a_sem,
    b_sem,
    out_sem,
    own_sem,
):
    zs, per_z, reps, extent, rb, jb, pieces = dims
    plane = per_z * reps
    width = extent // pieces
    nb = rb * jb
    keys = zs * plane

    f = lax.axis_index("fsdp")
    y = lax.axis_index("rep")
    z = f // per_z
    q = lax.rem(f, per_z)
    p = q * reps + y

    def at_z(other):
        return (other * per_z + q, y)

    def at_p(other):
        return (z * per_z + other // reps, lax.rem(other, reps))

    def at_y(other):
        return (f, other)

    barrier = pltpu.get_barrier_semaphore()

    def greet_z(k, carry):
        pl.semaphore_signal(barrier, inc=1, device_id=at_z(lax.rem(z + k, zs)), device_id_type=MESH)
        return carry

    def greet_p(k, carry):
        pl.semaphore_signal(barrier, inc=1, device_id=at_p(lax.rem(p + k, plane)), device_id_type=MESH)
        return carry

    lax.fori_loop(1, zs, greet_z, 0)
    lax.fori_loop(1, plane, greet_p, 0)

    own_copy = pltpu.make_async_copy(grads.at[y], own, local_sem.at[0])
    own_copy.start()
    left_copy = pltpu.make_async_copy(left.at[0], stats.at[0], local_sem.at[1])
    left_copy.start()
    right_copy = pltpu.make_async_copy(right.at[0], stats.at[1], local_sem.at[2])
    right_copy.start()

    pl.semaphore_wait(barrier, zs - 1 + plane - 1)

    def cols(h, j):
        return pl.ds(j * extent + h * width, width)

    for h in range(pieces):
        def send_y(k, carry):
            other = lax.rem(y + k, reps)
            for j in range(jb):
                pltpu.make_async_remote_copy(
                    src_ref=grads.at[other, :, cols(h, j)],
                    dst_ref=yrecv.at[h, k - 1, j],
                    send_sem=send_sem.at[0],
                    recv_sem=y_sem.at[h],
                    device_id=at_y(other),
                    device_id_type=MESH,
                ).start()
            return carry

        lax.fori_loop(1, reps, send_y, 0)

    rank_r = rank_row[...]
    rank_c = rank_col[...]
    owner_r = rank_r >> ORDER_BITS
    owner_c = rank_c >> ORDER_BITS
    before_r = (rank_c >= (owner_r << ORDER_BITS)) & (rank_c < rank_r)
    slot_r = jnp.sum(jnp.where(before_r, 1.0, 0.0), axis=0, keepdims=True).astype(jnp.int32)
    before_c = (rank_r >= (owner_c << ORDER_BITS)) & (rank_r < rank_c)
    slot_c = jnp.sum(jnp.where(before_c, 1.0, 0.0), axis=1, keepdims=True).astype(jnp.int32)
    key_r = owner_r * reps + slot_r
    key_c = owner_c * reps + slot_c
    to_key[...] = one_hot(lax.broadcasted_iota(jnp.int32, (keys, nb), 0) == key_r)
    to_block[...] = one_hot(lax.broadcasted_iota(jnp.int32, (nb, keys), 1) == key_c)
    row = lax.broadcasted_iota(jnp.int32, (keys, keys), 0)
    col = lax.broadcasted_iota(jnp.int32, (keys, keys), 1)
    z_bits = zs.bit_length() - 1
    p_bits = plane.bit_length() - 1
    to_slot[...] = one_hot(col == ((row & (zs - 1)) << p_bits) + (row >> z_bits))
    to_z[...] = one_hot(col == ((row & (plane - 1)) << z_bits) + (row >> p_bits))

    own_copy.wait()

    def z_far_first(k):
        away = zs // 2 - (k + 1) // 2
        away = jnp.where(lax.rem(k, 2) == 1, away, zs - away)
        return lax.rem(z + away, zs)

    for h in range(pieces):
        pltpu.make_async_copy(yrecv.at[h], yrecv.at[h], y_sem.at[h]).wait()
        parts = []
        for j in range(jb):
            total = own[:, j * extent + h * width : j * extent + (h + 1) * width].astype(F32)
            for k in range(reps - 1):
                total = total + yrecv[h, k, j].astype(F32)
            parts.append((total * (1.0 / reps)).astype(BF16))
        averaged = jnp.concatenate(parts, axis=0)
        zsend[h] = mm(to_key[...], averaged).astype(BF16).reshape(zs, plane, width)

        def send_z(k, carry):
            other = z_far_first(k)
            pltpu.make_async_remote_copy(
                src_ref=zsend.at[h, other],
                dst_ref=zrecv.at[h, z],
                send_sem=send_sem.at[1],
                recv_sem=z_sem.at[h],
                device_id=at_z(other),
                device_id_type=MESH,
            ).start()
            return carry

        lax.fori_loop(0, zs - 1, send_z, 0)
        zrecv[h, z] = zsend[h, z]

    for h in range(pieces):
        pltpu.make_async_copy(
            zrecv.at[h, pl.ds(0, zs - 1)], zrecv.at[h, pl.ds(0, zs - 1)], z_sem.at[h]
        ).wait()
        arrived = zrecv[h].reshape(keys, width)
        psend[h] = mm(to_slot[...], arrived).astype(BF16).reshape(plane, zs, width)

        def send_p(k, carry):
            other = lax.rem(p + k, plane)
            pltpu.make_async_remote_copy(
                src_ref=psend.at[h, other],
                dst_ref=precv.at[h, p],
                send_sem=send_sem.at[2],
                recv_sem=p_sem.at[h],
                device_id=at_p(other),
                device_id_type=MESH,
            ).start()
            return carry

        lax.fori_loop(1, plane, send_p, 0)
        precv[h, p] = psend[h, p]

    for h in range(pieces):
        pltpu.make_async_copy(
            precv.at[h, pl.ds(0, plane - 1)], precv.at[h, pl.ds(0, plane - 1)], p_sem.at[h]
        ).wait()
        arrived = precv[h].reshape(keys, width)
        gmat[:, h * width : (h + 1) * width] = mm(to_z[...], arrived).astype(BF16)

    left_copy.wait()
    right_copy.wait()
    g = gmat[...]
    dense = g.astype(F32)
    left_factor, left_rest = newton_root(stats[0] + mm_nt(g, g))
    right_factor, right_rest = newton_root(stats[1] + mm_tn(g, g))
    half = 1.5625 * dense + mm(left_rest.astype(BF16), g)
    shaped = 1.5625 * half + mm(half.astype(BF16), right_rest.astype(BF16))
    root_scale = jnp.sqrt(jnp.sqrt(left_factor)) * jnp.sqrt(jnp.sqrt(right_factor))
    count = 1.0 / (extent * extent)
    grad_rms = jnp.sqrt(jnp.sum(dense * dense) * count)
    shaped_rms = jnp.sqrt(jnp.sum(shaped * shaped) * count * (root_scale * root_scale) + 1e-06)
    pmat[...] = (shaped * (root_scale * (grad_rms / shaped_rms))).astype(BF16)

    for h in range(pieces):
        rows = pmat[:, h * width : (h + 1) * width]
        asend[h] = mm(to_slot[...], rows).astype(BF16).reshape(plane, zs, width)

        def send_a(k, carry):
            other = lax.rem(p + k, plane)
            pltpu.make_async_remote_copy(
                src_ref=asend.at[h, other],
                dst_ref=arecv.at[h, p],
                send_sem=send_sem.at[3],
                recv_sem=a_sem.at[h],
                device_id=at_p(other),
                device_id_type=MESH,
            ).start()
            return carry

        lax.fori_loop(1, plane, send_a, 0)
        arecv[h, p] = asend[h, p]

    for h in range(pieces):
        pltpu.make_async_copy(
            arecv.at[h, pl.ds(0, plane - 1)], arecv.at[h, pl.ds(0, plane - 1)], a_sem.at[h]
        ).wait()
        arrived = arecv[h].reshape(keys, width)
        bsend[h] = mm(to_z[...], arrived).astype(BF16).reshape(zs, plane, width)

        def send_b(k, carry):
            other = z_far_first(k)
            pltpu.make_async_remote_copy(
                src_ref=bsend.at[h, other],
                dst_ref=brecv.at[h, z],
                send_sem=send_sem.at[4],
                recv_sem=b_sem.at[h],
                device_id=at_z(other),
                device_id_type=MESH,
            ).start()
            return carry

        lax.fori_loop(0, zs - 1, send_b, 0)
        brecv[h, z] = bsend[h, z]

    for h in range(pieces):
        pltpu.make_async_copy(
            brecv.at[h, pl.ds(0, zs - 1)], brecv.at[h, pl.ds(0, zs - 1)], b_sem.at[h]
        ).wait()
        arrived = brecv[h].reshape(keys, width)
        vsend[h] = mm(to_block[...], arrived).astype(BF16).reshape(jb, rb, width)

        def send_out(k, carry):
            other = lax.rem(y + k, reps)
            for j in range(jb):
                pltpu.make_async_remote_copy(
                    src_ref=vsend.at[h, j],
                    dst_ref=out.at[y, :, cols(h, j)],
                    send_sem=send_sem.at[5],
                    recv_sem=out_sem,
                    device_id=at_y(other),
                    device_id_type=MESH,
                ).start()
            return carry

        lax.fori_loop(1, reps, send_out, 0)
        for j in range(jb):
            pltpu.make_async_copy(vsend.at[h, j], out.at[y, :, cols(h, j)], own_sem).start()

    pltpu.make_async_copy(vsend, vsend, own_sem).wait()
    others = pl.ds(0, reps - 1)
    pltpu.make_async_copy(out.at[others], out.at[others], out_sem).wait()
    pltpu.make_async_copy(yrecv, yrecv, send_sem.at[0]).wait()
    pltpu.make_async_copy(out.at[others], out.at[others], send_sem.at[5]).wait()
    for ref, count_, at in (
        (zsend, zs - 1, 1),
        (psend, plane - 1, 2),
        (asend, plane - 1, 3),
        (bsend, zs - 1, 4),
    ):
        sent = ref.at[:, pl.ds(0, count_)]
        pltpu.make_async_copy(sent, sent, send_sem.at[at]).wait()


def per_device(gradients, owner, left_stats, right_stats):
    reps = lax.axis_size("rep")
    owners = lax.axis_size("fsdp")
    rows, rb, width = gradients.shape[1:]
    extent = rows * owners
    jb = width // extent
    nb = rb * jb
    zs = owners // PER_Z
    plane = PER_Z * reps
    w = extent // PIECES
    keys = owners * reps
    assert rows == reps and keys == extent

    number = np.arange(nb, dtype=np.int32).reshape(rb, jb).T.reshape(nb)
    rank = (owner.reshape(rb, jb).T.reshape(nb) << ORDER_BITS) + number
    assert nb <= 1 << ORDER_BITS

    vmem = pl.BlockSpec(memory_space=pltpu.VMEM)
    anywhere = pl.BlockSpec(memory_space=pl.ANY)
    dma = pltpu.SemaphoreType.DMA
    return pl.pallas_call(
        functools.partial(kernel, (zs, PER_Z, reps, extent, rb, jb, PIECES)),
        out_shape=jax.ShapeDtypeStruct((rows, rb, width), BF16),
        in_specs=[anywhere, vmem, vmem, anywhere, anywhere],
        out_specs=anywhere,
        scratch_shapes=[
            pltpu.VMEM((rb, width), BF16),
            pltpu.VMEM((2, extent, extent), F32),
            pltpu.VMEM((PIECES, reps - 1, jb, rb, w), BF16),
            pltpu.VMEM((PIECES, zs, plane, w), BF16),
            pltpu.VMEM((PIECES, zs, plane, w), BF16),
            pltpu.VMEM((PIECES, plane, zs, w), BF16),
            pltpu.VMEM((PIECES, plane, zs, w), BF16),
            pltpu.VMEM((PIECES, plane, zs, w), BF16),
            pltpu.VMEM((PIECES, plane, zs, w), BF16),
            pltpu.VMEM((PIECES, zs, plane, w), BF16),
            pltpu.VMEM((PIECES, zs, plane, w), BF16),
            pltpu.VMEM((PIECES, jb, rb, w), BF16),
            pltpu.VMEM((keys, nb), BF16),
            pltpu.VMEM((nb, keys), BF16),
            pltpu.VMEM((keys, keys), BF16),
            pltpu.VMEM((keys, keys), BF16),
            pltpu.VMEM((extent, extent), BF16),
            pltpu.VMEM((extent, extent), BF16),
            dma((3,)),
            dma((6,)),
            dma((PIECES,)),
            dma((PIECES,)),
            dma((PIECES,)),
            dma((PIECES,)),
            dma((PIECES,)),
            dma,
            dma,
        ],
        compiler_params=pltpu.CompilerParams(
            collective_id=0, has_side_effects=True, vmem_limit_bytes=48 * 1024 * 1024
        ),
    )(gradients[0], rank.reshape(1, nb), rank.reshape(nb, 1), left_stats, right_stats)


def solution(mesh):
    placed = (
        P("rep", "fsdp", None, None),
        P(),
        P(("fsdp", "rep"), None, None),
        P(("fsdp", "rep"), None, None),
    )
    return jax.shard_map(
        per_device, mesh=mesh, in_specs=placed, out_specs=P("fsdp", None, None), check_vma=False
    )
```

time: 253 us -> 104 us (0.41)
  waiting for transfers between devices: 101 us -> 0 us
  Pallas kernels: 0 us -> 97.4 us
  blocking collectives: 88 us -> 0 us
  matrix products: 23.7 us -> 0 us
  between operations: 16.7 us -> 0.03 us
  other arithmetic: 9.59 us -> 0.68 us
  local copies, waits for them, and re-layouts: 13.5 us -> 5.27 us
    pallas_call x0 -> x1, Pallas kernels: none -> 97.4 us  [per_device(): pl.pallas_call(functools.partial(kernel, (zs, PER_Z, reps, extent, rb, jb...]
    all_to_all x2 -> x0, blocking collectives: 88 us -> none  [the longest x1 48.2 us: per_device(): lax.all_to_all(outgoing, 'fsdp', split_axis=1, concat_axis=0, tiled=True)]
    psum x1 -> x0, waiting for transfers between devices: 69.2 us -> none  [per_device(): lax.psum(own_rows.astype(jnp.float32).astype(jnp.bfloat16), 'rep')]
    all_gather x1 -> x0, waiting for transfers between devices: 31.4 us -> none  [per_device(): collected = lax.all_gather(returned[:, None], 'rep', axis=1, tiled=True)]
    dot_general x12 -> x0, matrix products: 23.7 us -> none  [the longest x10 21.3 us: exact_dot(): jnp.dot(lhs_mat, rhs_mat, precision=lax.Precision.HIGHEST, preferred_elem...]
    gather x4 -> x0, local copies, waits for them, and re-layouts: 6.27 us -> none  [the longest x3 5.24 us: per_device(): picked = jnp.take(flattened, slot_of * owners + owner, axis=1)]
    unnamed x9 -> x7, local copies, waits for them, and re-layouts: 1.68 us -> 4.86 us
    all_to_all x1 -> x0, other arithmetic: 3.18 us -> none  [per_device(): lax.all_to_all(update.reshape(extent, 1, extent), 'fsdp', split_axis=0, c...]
  transfers between devices with their start and end apart: 2 -> 0, of which waited for: 2 -> 0; matrix products, arithmetic and copies ran while one was open for 1% -> 0% of each run, Pallas kernels for 0% -> 0%
where the time goes in v1:
time: 104 us; the launch traced here: 103 us
  Pallas kernels  97.4 us (94%)
  local copies, waits for them, and re-layouts  5.27 us (5%)
    pallas_call x1, Pallas kernels, per_device(): pl.pallas_call(functools.partial(kernel, (zs, PER_Z, reps, extent, rb, jb...  97.4 us
    unnamed x7, local copies, waits for them, and re-layouts  4.86 us

profile of v1, /device:TPU:1, one launch (start us, length us, event | category | flops | bytes accessed | tf_op | source)
XLA Modules:
  0.0 103.3 jit_solution(2931201337405426119)
XLA Ops:
  0.0 0.7 iota_add_fusion
  0.7 0.1 reshape.19
  0.8 0.1 copy.6
  0.9 0.1 reshape.12.rank_row
  1.0 0.1 reshape.20.rank_col
  1.1 0.0 copy-start
  1.1 1.3 %copy-done = bf16[1,4,48,3584]{3,2,1,0:T(8,128)(2,1)S(1)} copy-done((bf16[1,4,48,3584]{3,2,1,0:T(8,128)(2,1)S(1)}, bf16[1,4,48,3584]{3,2,1,0:T(8,128)(2,1)}, u32[]{:S(2)}) %copy-start) | copy-done | bytes 1376280
  2.4 0.0 copy-start.1
  2.4 1.2 %copy-done.1 = f32[1,512,512]{2,1,0:T(8,128)S(1)} copy-done((f32[1,512,512]{2,1,0:T(8,128)S(1)}, f32[1,512,512]{2,1,0:T(8,128)}, u32[]{:S(2)}) %copy-start.1) | copy-done | bytes 1048600
  3.7 0.0 copy-start.2
  3.7 1.2 %copy-done.2 = f32[1,512,512]{2,1,0:T(8,128)S(1)} copy-done((f32[1,512,512]{2,1,0:T(8,128)S(1)}, f32[1,512,512]{2,1,0:T(8,128)}, u32[]{:S(2)}) %copy-start.2) | copy-done | bytes 1048600
  4.9 97.4 %shard_map.55 = bf16[4,48,3584]{2,1,0:T(8,128)(2,1)S(1)} custom-call(bf16[4,48,3584]{2,1,0:T(8,128)(2,1)S(1)} %bitcast.2, s32[1,336]{1,0:T(1,128)S(1)} %reshape.12.rank_row, s32[336,1]{1,0:T(8,128)S(1)} %reshape.20.rank_col, f32[1,512,512]{2,1,0:T(8,128)S(1)} %copy-done.1, f32[1,512,512]{2,1,0:T(8,128)S(1)} %copy-done.2), custom_call_target="tpu_custom_call" | custom-call | tf_op jit(solution)/shard_map/pallas_call | solution.py:340
  102.3 1.1 %copy.10 = bf16[4,48,3584]{2,1,0:T(8,128)(2,1)} copy(bf16[4,48,3584]{2,1,0:T(8,128)(2,1)S(1)} %shard_map.55) | data formatting | bytes 2752512
Async XLA Ops:
  1.1 1.3 %copy-start = (bf16[1,4,48,3584]{3,2,1,0:T(8,128)(2,1)S(1)}, bf16[1,4,48,3584]{3,2,1,0:T(8,128)(2,1)}, u32[]{:S(2)}) copy-start(bf16[1,4,48,3584]{3,2,1,0:T(8,128)(2,1)} %param.5) | copy-start | bytes 4128772
  2.4 1.2 %copy-start.1 = (f32[1,512,512]{2,1,0:T(8,128)S(1)}, f32[1,512,512]{2,1,0:T(8,128)}, u32[]{:S(2)}) copy-start(f32[1,512,512]{2,1,0:T(8,128)} %left.1) | copy-start | bytes 3145732
  3.7 1.2 %copy-start.2 = (f32[1,512,512]{2,1,0:T(8,128)S(1)}, f32[1,512,512]{2,1,0:T(8,128)}, u32[]{:S(2)}) copy-start(f32[1,512,512]{2,1,0:T(8,128)} %right.1) | copy-start | bytes 3145732

commit v2 on v0

v2 whole, which is shorter than its diff:
```python
import functools

import jax
import jax.numpy as jnp
from jax import lax
from jax.experimental import pallas as pl
from jax.experimental.pallas import tpu as pltpu
from jax.sharding import PartitionSpec as P

MESH = pl.DeviceIdType.MESH
CORES = 2
PER_Z = 8
LANES = 128
MOVES = (
    (2, 2), (1, 2), (3, 2), (2, 1), (2, 3), (1, 1), (3, 3), (1, 3),
    (3, 1), (2, 0), (0, 2), (1, 0), (3, 0), (0, 1), (0, 3), (0, 0),
)

F32 = jnp.float32
BF16 = jnp.bfloat16


def mm(lhs, rhs):
    return lax.dot_general(lhs, rhs, (((1,), (0,)), ((), ())), preferred_element_type=F32)


def mm_nt(lhs, rhs):
    return lax.dot_general(lhs, rhs, (((1,), (1,)), ((), ())), preferred_element_type=F32)


def mm_tn(lhs, rhs):
    return lax.dot_general(lhs, rhs, (((0,), (0,)), ((), ())), preferred_element_type=F32)


def one_hot(mask):
    return jnp.where(mask, 1.0, 0.0).astype(BF16)


def iota(shape, dim):
    return lax.broadcasted_iota(jnp.int32, shape, dim)


def newton_root(acc):
    factor = 2.5 / jnp.sqrt(jnp.sum(acc * acc))
    m = acc * factor
    mb = m.astype(BF16)
    q = mm(mb, mb) * 0.0625 - 0.625 * m
    t = 1.5625 * m + mm(q.astype(BF16), mb)
    r = 1.25 * q - 0.25 * t
    rest = -0.3125 * m - 0.25 * (1.953125 * t + mm(r.astype(BF16), t.astype(BF16)))
    return factor, rest


def wait_bytes(ref, sem):
    pltpu.make_async_copy(ref, ref, sem).wait()


def kernel(dims, owner, grads, left, right, out, s):
    zs, reps, extent, rb, jb, groups, lanes = dims
    xs = PER_Z // CORES
    plane = PER_Z * reps
    nb = rb * jb
    keys = zs * plane

    f = lax.axis_index("fsdp")
    y = lax.axis_index("rep")
    z = f // PER_Z
    q = lax.rem(f, PER_Z)
    x, c = q // CORES, lax.rem(q, CORES)
    p = q * reps + y

    barrier = pltpu.get_barrier_semaphore()

    def greet_z(k, carry):
        to = (lax.rem(z + k, zs) * PER_Z + q, y)
        pl.semaphore_signal(barrier, inc=1, device_id=to, device_id_type=MESH)
        return carry

    def greet_p(k, carry):
        other = lax.rem(p + k, plane)
        to = (z * PER_Z + other // reps, lax.rem(other, reps))
        pl.semaphore_signal(barrier, inc=1, device_id=to, device_id_type=MESH)
        return carry

    rows_copy = pltpu.make_async_copy(grads, s["rows"], s["local_sem"].at[0])
    rows_copy.start()
    lax.fori_loop(1, zs, greet_z, 0)
    lax.fori_loop(1, plane, greet_p, 0)
    left_copy = pltpu.make_async_copy(left.at[0], s["stats"].at[0], s["local_sem"].at[1])
    left_copy.start()
    right_copy = pltpu.make_async_copy(right.at[0], s["stats"].at[1], s["local_sem"].at[2])
    right_copy.start()

    def number(at):
        j = sum(jnp.where(at >= rb * t, 1, 0) for t in range(1, jb))
        return (at - j * rb) * jb + j

    z_bits = zs.bit_length() - 1
    p_bits = plane.bit_length() - 1

    def place(key):
        return ((key & (plane - 1)) << z_bits) + (key >> p_bits)

    blocks = (nb, nb)
    b0, b1 = iota(blocks, 0), iota(blocks, 1)
    owner_r = owner[...].reshape(1, nb)
    owner_c = jnp.sum(jnp.where(b0 == b1, owner_r, 0).astype(F32), axis=1, keepdims=True).astype(jnp.int32)
    same = owner_c == owner_r
    slot_r = jnp.sum(jnp.where(same & (b0 < b1), 1.0, 0.0), axis=0, keepdims=True).astype(jnp.int32)
    key_of = one_hot(iota((keys, nb), 0) == place(owner_r * reps + slot_r))
    s["to_key"][...] = mm(key_of, one_hot(b0 == number(b1))).astype(BF16)

    def gather(h):
        for a in range(reps):
            parts = [s["rows"][a, :, j * extent + h * lanes : j * extent + (h + 1) * lanes] for j in range(jb)]
            picked = mm(s["to_key"][...], jnp.concatenate(parts, axis=0))
            s["ysend"][h, :, a] = picked.astype(BF16).reshape(plane, zs, lanes)

    def plane_sends(source, dest, stage, h):
        def send(core, move):
            qx = lax.rem(x + move[0], xs) * CORES + lax.rem(c + core, CORES)
            py = lax.rem(y + move[1], reps)
            pltpu.make_async_remote_copy(
                src_ref=source(qx, py),
                dst_ref=dest.at[h, p],
                send_sem=s["send_sem"].at[stage],
                recv_sem=s["recv_sem"].at[stage, h],
                device_id=(z * PER_Z + qx, py),
                device_id_type=MESH,
            ).start()

        def step(core, carry):
            for move in MOVES:
                if move != (0, 0):
                    send(core, move)
                else:
                    pl.when(core > 0)(functools.partial(send, core, move))
            return carry

        lax.fori_loop(0, CORES, step, 0)

    def z_send(source, dest, stage, h, other):
        pltpu.make_async_remote_copy(
            src_ref=source.at[h, other],
            dst_ref=dest.at[h, z],
            send_sem=s["send_sem"].at[stage],
            recv_sem=s["recv_sem"].at[stage, h],
            device_id=(other * PER_Z + q, y),
            device_id_type=MESH,
        ).start()

    others_z = pl.ds(0, zs - 1)
    others_p = pl.ds(0, plane - 1)

    rows_copy.wait()
    gather(0)
    pl.semaphore_wait(barrier, zs - 1 + plane - 1)
    for h in range(groups):
        if h > 0:
            gather(h)
        plane_sends(lambda qx, py: s["ysend"].at[h, qx * reps + py], s["yrecv"], 0, h)
        s["yrecv"][h, p] = s["ysend"][h, p]

    row, col = iota((keys, keys), 0), iota((keys, keys), 1)
    s["to_z"][...] = one_hot(col == ((row & (plane - 1)) << z_bits) + (row >> p_bits))

    for h in range(groups):
        wait_bytes(s["yrecv"].at[h, others_p], s["recv_sem"].at[0, h])
        parts = []
        for k in range(PER_Z):
            total = s["yrecv"][h, k * reps].astype(F32)
            for other in range(1, reps):
                total = total + s["yrecv"][h, k * reps + other].astype(F32)
            parts.append((total * (1.0 / reps)).astype(BF16).reshape(reps * zs, lanes))
        averaged = jnp.concatenate(parts, axis=0)
        s["zsend"][h] = mm(s["to_z"][...], averaged).astype(BF16).reshape(zs, plane, lanes)

        def step(k, carry):
            away = zs // 2 - (k + 1) // 2
            odd = lax.rem(k, 2)
            z_send(s["zsend"], s["zrecv"], 1, h, lax.rem(z + odd * away + (1 - odd) * (zs - away), zs))
            return carry

        lax.fori_loop(0, zs - 1, step, 0)
        s["zrecv"][h, z] = s["zsend"][h, z]

    slot_c = jnp.sum(jnp.where(same & (b1 < b0), 1.0, 0.0), axis=1, keepdims=True).astype(jnp.int32)
    of_key = one_hot(iota((nb, keys), 1) == place(owner_c * reps + slot_c))
    s["to_block"][...] = mm(one_hot(b1 == number(b0)), of_key).astype(BF16)
    s["to_slot"][...] = one_hot(col == ((row & (zs - 1)) << p_bits) + (row >> z_bits))

    left_copy.wait()
    right_copy.wait()
    for h in range(groups):
        wait_bytes(s["zrecv"].at[h, others_z], s["recv_sem"].at[1, h])
        s["gmat"][:, h * lanes : (h + 1) * lanes] = s["zrecv"][h].reshape(keys, lanes)
    g = s["gmat"][...]
    dense = g.astype(F32)
    left_factor, left_rest = newton_root(s["stats"][0] + mm_nt(g, g))
    right_factor, right_rest = newton_root(s["stats"][1] + mm_tn(g, g))
    half = 1.5625 * dense + mm(left_rest.astype(BF16), g)
    shaped = 1.5625 * half + mm(half.astype(BF16), right_rest.astype(BF16))
    root_scale = jnp.sqrt(jnp.sqrt(left_factor)) * jnp.sqrt(jnp.sqrt(right_factor))
    mean = 1.0 / (extent * extent)
    grad_rms = jnp.sqrt(jnp.sum(dense * dense) * mean)
    shaped_rms = jnp.sqrt(jnp.sum(shaped * shaped) * mean * (root_scale * root_scale) + 1e-06)
    update = (shaped * (root_scale * (grad_rms / shaped_rms))).astype(BF16)
    for h in range(groups):
        s["bsend"][h] = update[:, h * lanes : (h + 1) * lanes].reshape(zs, plane, lanes)

    for h in range(groups):

        def step(k, carry):
            other = lax.rem(k, 2) * (zs // 2) + k // 2
            pl.when(other != z)(functools.partial(z_send, s["bsend"], s["brecv"], 2, h, other))
            return carry

        lax.fori_loop(0, zs, step, 0)
        s["brecv"][h, z] = s["bsend"][h, z]

    def back(h):
        wait_bytes(s["brecv"].at[h, others_z], s["recv_sem"].at[2, h])
        rows = mm(s["to_slot"][...], s["brecv"][h].reshape(keys, lanes)).astype(BF16)
        s["psend"][h] = rows.reshape(PER_Z, reps, zs, lanes)
        plane_sends(lambda qx, py: s["psend"].at[h, qx], s["precv"], 3, h)
        s["precv"][h, p] = s["psend"][h, q]

    def write(h):
        wait_bytes(s["precv"].at[h, others_p], s["recv_sem"].at[3, h])
        for a in range(reps):
            rows = mm(s["to_block"][...], s["precv"][h, :, a].reshape(keys, lanes)).astype(BF16)
            for j in range(jb):
                at = j * extent + h * lanes
                s["rows"][a, :, at : at + lanes] = rows[j * rb : (j + 1) * rb]
        for j in range(jb):
            at = pl.ds(j * extent + h * lanes, lanes)
            pltpu.make_async_copy(s["rows"].at[:, :, at], out.at[:, :, at], s["local_sem"].at[3]).start()

    for h in range(groups):
        back(h)
        if h > 0:
            write(h - 1)
    write(groups - 1)

    wait_bytes(s["rows"], s["local_sem"].at[3])
    wait_bytes(s["ysend"].at[:, others_p], s["send_sem"].at[0])
    wait_bytes(s["zsend"].at[:, others_z], s["send_sem"].at[1])
    wait_bytes(s["bsend"].at[:, others_z], s["send_sem"].at[2])
    wait_bytes(s["precv"].at[:, others_p], s["send_sem"].at[3])


def per_device(gradients, owner, left_stats, right_stats):
    reps = lax.axis_size("rep")
    owners = lax.axis_size("fsdp")
    rows, rb, width = gradients.shape[1:]
    extent = rows * owners
    jb = width // extent
    nb = rb * jb
    zs = owners // PER_Z
    plane = PER_Z * reps
    groups = extent // LANES
    keys = owners * reps
    assert rows == reps and keys == extent

    vmem = pl.BlockSpec(memory_space=pltpu.VMEM)
    hbm = pl.BlockSpec(memory_space=pltpu.HBM)
    dma = pltpu.SemaphoreType.DMA
    by_z = pltpu.VMEM((groups, zs, plane, LANES), BF16)
    by_place = pltpu.VMEM((groups, plane, rows, zs, LANES), BF16)
    scratch = dict(
        rows=pltpu.VMEM((rows, rb, width), BF16),
        stats=pltpu.VMEM((2, extent, extent), F32),
        ysend=by_place,
        yrecv=by_place,
        zsend=by_z,
        zrecv=by_z,
        bsend=by_z,
        brecv=by_z,
        psend=pltpu.VMEM((groups, PER_Z, rows, zs, LANES), BF16),
        precv=by_place,
        to_key=pltpu.VMEM((keys, nb), BF16),
        to_block=pltpu.VMEM((nb, keys), BF16),
        to_slot=pltpu.VMEM((keys, keys), BF16),
        to_z=pltpu.VMEM((keys, keys), BF16),
        gmat=pltpu.VMEM((extent, extent), BF16),
        local_sem=dma((4,)),
        send_sem=dma((4,)),
        recv_sem=dma((4, groups)),
    )
    return pl.pallas_call(
        functools.partial(kernel, (zs, reps, extent, rb, jb, groups, LANES)),
        out_shape=jax.ShapeDtypeStruct((rows, rb, width), BF16),
        in_specs=[vmem, hbm, hbm, hbm],
        out_specs=pl.BlockSpec(memory_space=pl.ANY),
        scratch_shapes=[scratch],
        compiler_params=pltpu.CompilerParams(
            collective_id=0, has_side_effects=True, vmem_limit_bytes=60 * 1024 * 1024
        ),
    )(owner, gradients[0], left_stats, right_stats)


def solution(mesh):
    placed = (
        P("rep", "fsdp", None, None),
        P(),
        P(("fsdp", "rep"), None, None),
        P(("fsdp", "rep"), None, None),
    )
    return jax.shard_map(
        per_device, mesh=mesh, in_specs=placed, out_specs=P("fsdp", None, None), check_vma=False
    )
```

time: 253 us -> 94 us (0.37)
  waiting for transfers between devices: 101 us -> 0 us
  Pallas kernels: 0 us -> 91.3 us
  blocking collectives: 88 us -> 0 us
  matrix products: 23.7 us -> 0 us
  between operations: 16.7 us -> 0.01 us
  local copies, waits for them, and re-layouts: 13.5 us -> 2.51 us
  other arithmetic: 9.59 us -> 0 us
    pallas_call x0 -> x1, Pallas kernels: none -> 91.3 us  [per_device(): pl.pallas_call(functools.partial(kernel, (zs, reps, extent, rb, jb, group...]
    all_to_all x2 -> x0, blocking collectives: 88 us -> none  [the longest x1 48.2 us: per_device(): lax.all_to_all(outgoing, 'fsdp', split_axis=1, concat_axis=0, tiled=True)]
    psum x1 -> x0, waiting for transfers between devices: 69.2 us -> none  [per_device(): lax.psum(own_rows.astype(jnp.float32).astype(jnp.bfloat16), 'rep')]
    all_gather x1 -> x0, waiting for transfers between devices: 31.4 us -> none  [per_device(): collected = lax.all_gather(returned[:, None], 'rep', axis=1, tiled=True)]
    dot_general x12 -> x0, matrix products: 23.7 us -> none  [the longest x10 21.3 us: exact_dot(): jnp.dot(lhs_mat, rhs_mat, precision=lax.Precision.HIGHEST, preferred_elem...]
    gather x4 -> x0, local copies, waits for them, and re-layouts: 6.27 us -> none  [the longest x3 5.24 us: per_device(): picked = jnp.take(flattened, slot_of * owners + owner, axis=1)]
    reshape x4 -> x0, local copies, waits for them, and re-layouts: 3.18 us -> none  [the longest x2 2.54 us: per_device(): averaged.reshape(row_count, blocks, extent)]
    all_to_all x1 -> x0, other arithmetic: 3.18 us -> none  [per_device(): lax.all_to_all(update.reshape(extent, 1, extent), 'fsdp', split_axis=0, c...]
  transfers between devices with their start and end apart: 2 -> 0, of which waited for: 2 -> 0; matrix products, arithmetic and copies ran while one was open for 1% -> 0% of each run, Pallas kernels for 0% -> 0%
where the time goes in v2:
time: 94 us; the launch traced here: 93.9 us
  Pallas kernels  91.3 us (97%)
  local copies, waits for them, and re-layouts  2.51 us (3%)
    pallas_call x1, Pallas kernels, per_device(): pl.pallas_call(functools.partial(kernel, (zs, reps, extent, rb, jb, group...  91.3 us
    unnamed x1, local copies, waits for them, and re-layouts  2.51 us

profile of v2, /device:TPU:1, one launch (start us, length us, event | category | flops | bytes accessed | tf_op | source)
XLA Modules:
  0.0 93.9 jit_solution(1518153871018584162)
XLA Ops:
  0.0 91.3 %shard_map.46 = bf16[4,48,3584]{2,1,0:T(8,128)(2,1)} custom-call(s32[336]{0:T(512)} %owner.1, bf16[4,48,3584]{2,1,0:T(8,128)(2,1)} %bitcast.1, f32[1,512,512]{2,1,0:T(8,128)} %left.1, f32[1,512,512]{2,1,0:T(8,128)} %right.1), custom_call_target="tpu_custom_call" | custom-call | tf_op jit(solution)/shard_map/pallas_call | solution.py:290
  91.4 2.5 %copy.6 = bf16[4,48,3584]{2,1,0:T(8,128)(2,1)} copy(bf16[4,48,3584]{2,1,0:T(8,128)(2,1)} %shard_map.46) | data formatting | bytes 2752512

commit v3 on v2

--- a/solution.py
+++ b/solution.py
@@ -91,15 +91,22 @@
     right_copy = pltpu.make_async_copy(right.at[0], s["stats"].at[1], s["local_sem"].at[2])
     right_copy.start()
 
+    near = zs // 2
+
+    def rank(away):
+        return jnp.where(away < near, zs - 1 - 2 * away, 2 * (away - near))
+
     def number(at):
         j = sum(jnp.where(at >= rb * t, 1, 0) for t in range(1, jb))
         return (at - j * rb) * jb + j
 
-    z_bits = zs.bit_length() - 1
     p_bits = plane.bit_length() - 1
+    n_bits = near.bit_length() - 1
+    part = plane * near
 
     def place(key):
-        return ((key & (plane - 1)) << z_bits) + (key >> p_bits)
+        r = rank(((key >> p_bits) - z) & (zs - 1))
+        return (r >> n_bits) * part + ((key & (plane - 1)) << n_bits) + (r & (near - 1))
 
     blocks = (nb, nb)
     b0, b1 = iota(blocks, 0), iota(blocks, 1)
@@ -110,21 +117,23 @@
     key_of = one_hot(iota((keys, nb), 0) == place(owner_r * reps + slot_r))
     s["to_key"][...] = mm(key_of, one_hot(b0 == number(b1))).astype(BF16)
 
-    def gather(h):
+    def gather(h, half):
+        key_rows = s["to_key"][half * part : (half + 1) * part]
+        picked = []
         for a in range(reps):
             parts = [s["rows"][a, :, j * extent + h * lanes : j * extent + (h + 1) * lanes] for j in range(jb)]
-            picked = mm(s["to_key"][...], jnp.concatenate(parts, axis=0))
-            s["ysend"][h, :, a] = picked.astype(BF16).reshape(plane, zs, lanes)
-
-    def plane_sends(source, dest, stage, h):
+            picked.append(mm(key_rows, jnp.concatenate(parts, axis=0)).reshape(plane, near, lanes))
+        s["ysend"][h, half] = jnp.concatenate(picked, axis=1).astype(BF16)
+
+    def plane_sends(source, dest, stage, h, half):
         def send(core, move):
             qx = lax.rem(x + move[0], xs) * CORES + lax.rem(c + core, CORES)
             py = lax.rem(y + move[1], reps)
             pltpu.make_async_remote_copy(
                 src_ref=source(qx, py),
-                dst_ref=dest.at[h, p],
+                dst_ref=dest.at[h, half, p],
                 send_sem=s["send_sem"].at[stage],
-                recv_sem=s["recv_sem"].at[stage, h],
+                recv_sem=s["recv_sem"].at[stage, h, half],
                 device_id=(z * PER_Z + qx, py),
                 device_id_type=MESH,
             ).start()
@@ -139,12 +148,12 @@
 
         lax.fori_loop(0, CORES, step, 0)
 
-    def z_send(source, dest, stage, h, other):
+    def z_send(source, dest, stage, sem, other):
         pltpu.make_async_remote_copy(
-            src_ref=source.at[h, other],
-            dst_ref=dest.at[h, z],
+            src_ref=source,
+            dst_ref=dest,
             send_sem=s["send_sem"].at[stage],
-            recv_sem=s["recv_sem"].at[stage, h],
+            recv_sem=sem,
             device_id=(other * PER_Z + q, y),
             device_id_type=MESH,
         ).start()
@@ -152,47 +161,58 @@
     others_z = pl.ds(0, zs - 1)
     others_p = pl.ds(0, plane - 1)
 
-    rows_copy.wait()
-    gather(0)
-    pl.semaphore_wait(barrier, zs - 1 + plane - 1)
-    for h in range(groups):
-        if h > 0:
-            gather(h)
-        plane_sends(lambda qx, py: s["ysend"].at[h, qx * reps + py], s["yrecv"], 0, h)
-        s["yrecv"][h, p] = s["ysend"][h, p]
-
-    row, col = iota((keys, keys), 0), iota((keys, keys), 1)
-    s["to_z"][...] = one_hot(col == ((row & (plane - 1)) << z_bits) + (row >> p_bits))
-
-    for h in range(groups):
-        wait_bytes(s["yrecv"].at[h, others_p], s["recv_sem"].at[0, h])
+    def to_place(h, half):
+        plane_sends(lambda qx, py: s["ysend"].at[h, half, qx * reps + py], s["yrecv"], 0, h, half)
+        s["yrecv"][h, half, p] = s["ysend"][h, half, p]
+
+    def to_owner(h, half):
+        wait_bytes(s["yrecv"].at[h, half, others_p], s["recv_sem"].at[0, h, half])
         parts = []
         for k in range(PER_Z):
-            total = s["yrecv"][h, k * reps].astype(F32)
+            total = s["yrecv"][h, half, k * reps].astype(F32)
             for other in range(1, reps):
-                total = total + s["yrecv"][h, k * reps + other].astype(F32)
-            parts.append((total * (1.0 / reps)).astype(BF16).reshape(reps * zs, lanes))
+                total = total + s["yrecv"][h, half, k * reps + other].astype(F32)
+            parts.append((total * (1.0 / reps)).astype(BF16))
         averaged = jnp.concatenate(parts, axis=0)
-        s["zsend"][h] = mm(s["to_z"][...], averaged).astype(BF16).reshape(zs, plane, lanes)
+        s["zsend"][h, half] = mm(s["to_z"][...], averaged).astype(BF16).reshape(near, plane, lanes)
 
         def step(k, carry):
-            away = zs // 2 - (k + 1) // 2
-            odd = lax.rem(k, 2)
-            z_send(s["zsend"], s["zrecv"], 1, h, lax.rem(z + odd * away + (1 - odd) * (zs - away), zs))
+            r = half * near + k
+            odd = lax.rem(r, 2)
+            away = near - (r + 1) // 2
+            other = lax.rem(z + odd * away + (1 - odd) * (zs - away), zs)
+            z_send(s["zsend"].at[h, half, k], s["zrecv"].at[h, z], 1, s["recv_sem"].at[1, h, 0], other)
             return carry
 
-        lax.fori_loop(0, zs - 1, step, 0)
-        s["zrecv"][h, z] = s["zsend"][h, z]
+        lax.fori_loop(0, near - half, step, 0)
+        if half == 1:
+            s["zrecv"][h, z] = s["zsend"][h, 1, near - 1]
+
+    rows_copy.wait()
+    gather(0, 0)
+    pl.semaphore_wait(barrier, zs - 1 + plane - 1)
+    to_place(0, 0)
+    row, col = iota((part, part), 0), iota((part, part), 1)
+    s["to_z"][...] = one_hot(col == ((row & (plane - 1)) << n_bits) + (row >> p_bits))
+    for h in range(1, groups):
+        gather(h, 0)
+        to_place(h, 0)
+    for h in range(groups):
+        gather(h, 1)
+        to_owner(h, 0)
+        to_place(h, 1)
+    for h in range(groups):
+        to_owner(h, 1)
 
     slot_c = jnp.sum(jnp.where(same & (b1 < b0), 1.0, 0.0), axis=1, keepdims=True).astype(jnp.int32)
     of_key = one_hot(iota((nb, keys), 1) == place(owner_c * reps + slot_c))
     s["to_block"][...] = mm(one_hot(b1 == number(b0)), of_key).astype(BF16)
-    s["to_slot"][...] = one_hot(col == ((row & (zs - 1)) << p_bits) + (row >> z_bits))
+    s["to_place"][...] = one_hot(col == ((row & (near - 1)) << p_bits) + (row >> n_bits))
 
     left_copy.wait()
     right_copy.wait()
     for h in range(groups):
-        wait_bytes(s["zrecv"].at[h, others_z], s["recv_sem"].at[1, h])
+        wait_bytes(s["zrecv"].at[h, others_z], s["recv_sem"].at[1, h, 0])
         s["gmat"][:, h * lanes : (h + 1) * lanes] = s["zrecv"][h].reshape(keys, lanes)
     g = s["gmat"][...]
     dense = g.astype(F32)
@@ -208,27 +228,48 @@
     for h in range(groups):
         s["bsend"][h] = update[:, h * lanes : (h + 1) * lanes].reshape(zs, plane, lanes)
 
-    for h in range(groups):
-
-        def step(k, carry):
-            other = lax.rem(k, 2) * (zs // 2) + k // 2
-            pl.when(other != z)(functools.partial(z_send, s["bsend"], s["brecv"], 2, h, other))
+    def back_z(h, half):
+        def send(other, r):
+            z_send(s["bsend"].at[h, other], s["brecv"].at[h, half, r], 2, s["recv_sem"].at[2, h, half], other)
+
+        def near_step(k, carry):
+            r = zs - 2 - k
+            odd = lax.rem(r, 2)
+            away = near - (r + 1) // 2
+            send(lax.rem(z + odd * (zs - away) + (1 - odd) * away, zs), r - near)
             return carry
 
-        lax.fori_loop(0, zs, step, 0)
-        s["brecv"][h, z] = s["bsend"][h, z]
-
-    def back(h):
-        wait_bytes(s["brecv"].at[h, others_z], s["recv_sem"].at[2, h])
-        rows = mm(s["to_slot"][...], s["brecv"][h].reshape(keys, lanes)).astype(BF16)
-        s["psend"][h] = rows.reshape(PER_Z, reps, zs, lanes)
-        plane_sends(lambda qx, py: s["psend"].at[h, qx], s["precv"], 3, h)
-        s["precv"][h, p] = s["psend"][h, q]
+        def far_step(k, carry):
+            other = lax.rem(k, 2) * near + k // 2
+            r = rank(lax.rem(z - other + zs, zs))
+            pl.when(r < near)(functools.partial(send, other, r))
+            return carry
+
+        if half == 1:
+            lax.fori_loop(0, near - 1, near_step, 0)
+            s["brecv"][h, 1, near - 1] = s["bsend"][h, z]
+        else:
+            lax.fori_loop(0, zs, far_step, 0)
+
+    for half in (1, 0):
+        for h in range(groups):
+            back_z(h, half)
+
+    def back(h, half):
+        wait_bytes(s["brecv"].at[h, half, pl.ds(0, near - half)], s["recv_sem"].at[2, h, half])
+        rows = mm(s["to_place"][...], s["brecv"][h, half].reshape(part, lanes)).astype(BF16)
+        s["psend"][h, half] = rows.reshape(PER_Z, reps * near, lanes)
+        plane_sends(lambda qx, py: s["psend"].at[h, half, qx], s["precv"], 3, h, half)
+        s["precv"][h, half, p] = s["psend"][h, half, q]
 
     def write(h):
-        wait_bytes(s["precv"].at[h, others_p], s["recv_sem"].at[3, h])
+        pieces = []
+        for half in range(2):
+            wait_bytes(s["precv"].at[h, half, others_p], s["recv_sem"].at[3, h, half])
+            pieces.append(s["precv"][h, half].astype(F32))
         for a in range(reps):
-            rows = mm(s["to_block"][...], s["precv"][h, :, a].reshape(keys, lanes)).astype(BF16)
+            at_a = [piece[:, a * near : (a + 1) * near].reshape(part, lanes) for piece in pieces]
+            rows = mm(s["to_block"][...], jnp.concatenate(at_a, axis=0).astype(BF16)).astype(BF16)
             for j in range(jb):
                 at = j * extent + h * lanes
                 s["rows"][a, :, at : at + lanes] = rows[j * rb : (j + 1) * rb]
@@ -237,16 +278,18 @@
             pltpu.make_async_copy(s["rows"].at[:, :, at], out.at[:, :, at], s["local_sem"].at[3]).start()
 
     for h in range(groups):
-        back(h)
+        back(h, 1)
+    for h in range(groups):
+        back(h, 0)
         if h > 0:
             write(h - 1)
     write(groups - 1)
 
     wait_bytes(s["rows"], s["local_sem"].at[3])
-    wait_bytes(s["ysend"].at[:, others_p], s["send_sem"].at[0])
-    wait_bytes(s["zsend"].at[:, others_z], s["send_sem"].at[1])
+    wait_bytes(s["ysend"].at[:, :, others_p], s["send_sem"].at[0])
+    wait_bytes(s["zrecv"].at[:, others_z], s["send_sem"].at[1])
     wait_bytes(s["bsend"].at[:, others_z], s["send_sem"].at[2])
-    wait_bytes(s["precv"].at[:, others_p], s["send_sem"].at[3])
+    wait_bytes(s["precv"].at[:, :, others_p], s["send_sem"].at[3])
 
 
 def per_device(gradients, owner, left_stats, right_stats):
@@ -266,26 +309,27 @@
     hbm = pl.BlockSpec(memory_space=pltpu.HBM)
     dma = pltpu.SemaphoreType.DMA
     by_z = pltpu.VMEM((groups, zs, plane, LANES), BF16)
-    by_place = pltpu.VMEM((groups, plane, rows, zs, LANES), BF16)
+    by_half = pltpu.VMEM((groups, 2, zs // 2, plane, LANES), BF16)
+    by_place = pltpu.VMEM((groups, 2, plane, rows * zs // 2, LANES), BF16)
     scratch = dict(
         rows=pltpu.VMEM((rows, rb, width), BF16),
         stats=pltpu.VMEM((2, extent, extent), F32),
         ysend=by_place,
         yrecv=by_place,
-        zsend=by_z,
+        zsend=by_half,
         zrecv=by_z,
         bsend=by_z,
-        brecv=by_z,
-        psend=pltpu.VMEM((groups, PER_Z, rows, zs, LANES), BF16),
+        brecv=by_half,
+        psend=pltpu.VMEM((groups, 2, PER_Z, rows * zs // 2, LANES), BF16),
         precv=by_place,
         to_key=pltpu.VMEM((keys, nb), BF16),
         to_block=pltpu.VMEM((nb, keys), BF16),
-        to_slot=pltpu.VMEM((keys, keys), BF16),
-        to_z=pltpu.VMEM((keys, keys), BF16),
+        to_place=pltpu.VMEM((keys // 2, keys // 2), BF16),
+        to_z=pltpu.VMEM((keys // 2, keys // 2), BF16),
         gmat=pltpu.VMEM((extent, extent), BF16),
         local_sem=dma((4,)),
         send_sem=dma((4,)),
-        recv_sem=dma((4, groups)),
+        recv_sem=dma((4, groups, 2)),
     )
     return pl.pallas_call(
         functools.partial(kernel, (zs, reps, extent, rb, jb, groups, LANES)),

time: 94 us -> 92.1 us (0.980)
  Pallas kernels: 91.3 us -> 89.1 us
    pallas_call x1, Pallas kernels: 91.3 us -> 89.1 us  [per_device(): pl.pallas_call(functools.partial(kernel, (zs, reps, extent, rb, jb, group...]
where the time goes in v3:
time: 92.1 us; the launch traced here: 91.6 us
  Pallas kernels  89.1 us (97%)
  local copies, waits for them, and re-layouts  2.51 us (3%)
    pallas_call x1, Pallas kernels, per_device(): pl.pallas_call(functools.partial(kernel, (zs, reps, extent, rb, jb, group...  89.1 us
    unnamed x1, local copies, waits for them, and re-layouts  2.51 us

profile of v3, /device:TPU:1, one launch (start us, length us, event | category | flops | bytes accessed | tf_op | source)
XLA Modules:
  0.0 91.6 jit_solution(13753389509488960003)
XLA Ops:
  0.0 89.1 %shard_map.46 = bf16[4,48,3584]{2,1,0:T(8,128)(2,1)} custom-call(s32[336]{0:T(512)} %owner.1, bf16[4,48,3584]{2,1,0:T(8,128)(2,1)} %bitcast.1, f32[1,512,512]{2,1,0:T(8,128)} %left.1, f32[1,512,512]{2,1,0:T(8,128)} %right.1), custom_call_target="tpu_custom_call" | custom-call | tf_op jit(solution)/shard_map/pallas_call | solution.py:334
  89.1 2.5 %copy.6 = bf16[4,48,3584]{2,1,0:T(8,128)(2,1)} copy(bf16[4,48,3584]{2,1,0:T(8,128)(2,1)} %shard_map.46) | data formatting | bytes 2752512

commit v4 on v3

--- a/solution.py
+++ b/solution.py
@@ -103,6 +103,8 @@
     p_bits = plane.bit_length() - 1
     n_bits = near.bit_length() - 1
     part = plane * near
+    few = near // 2
+    sizes = (near, few, few)
 
     def place(key):
         r = rank(((key >> p_bits) - z) & (zs - 1))
@@ -114,26 +116,47 @@
     owner_c = jnp.sum(jnp.where(b0 == b1, owner_r, 0).astype(F32), axis=1, keepdims=True).astype(jnp.int32)
     same = owner_c == owner_r
     slot_r = jnp.sum(jnp.where(same & (b0 < b1), 1.0, 0.0), axis=0, keepdims=True).astype(jnp.int32)
-    key_of = one_hot(iota((keys, nb), 0) == place(owner_r * reps + slot_r))
-    s["to_key"][...] = mm(key_of, one_hot(b0 == number(b1))).astype(BF16)
-
-    def gather(h, half):
-        key_rows = s["to_key"][half * part : (half + 1) * part]
-        picked = []
+    key_r = owner_r * reps + slot_r
+    swap = one_hot(b0 == number(b1))
+
+    def pick(r, at, use):
+        away = near - ((r + 1) >> 1)
+        away = jnp.where((r & 1) == 1, away, zs - away)
+        wanted = ((z + away) & (zs - 1)) * plane + at
+        return mm(one_hot((wanted == key_r) & use), swap).astype(BF16)
+
+    at_far = iota((part, 1), 0)
+    s["to_far"][...] = pick(at_far & (near - 1), at_far >> n_bits, at_far >= 0)
+
+    def fill_near():
+        for quarter in range(2):
+            r = near + quarter * few + (at_far & (few - 1))
+            first = (at_far & (near - 1)) < few
+            s["to_near"][quarter, 0] = pick(r, at_far >> n_bits, first)
+            s["to_near"][quarter, 1] = pick(r, at_far >> n_bits, jnp.logical_not(first))
+
+    def gather(h, k):
+        rows = []
         for a in range(reps):
             parts = [s["rows"][a, :, j * extent + h * lanes : j * extent + (h + 1) * lanes] for j in range(jb)]
-            picked.append(mm(key_rows, jnp.concatenate(parts, axis=0)).reshape(plane, near, lanes))
-        s["ysend"][h, half] = jnp.concatenate(picked, axis=1).astype(BF16)
-
-    def plane_sends(source, dest, stage, h, half):
+            rows.append(jnp.concatenate(parts, axis=0))
+        if k == 0:
+            picked = [mm(s["to_far"][...], row) for row in rows]
+        else:
+            one, two = s["to_near"][k - 1, 0], s["to_near"][k - 1, 1]
+            picked = [mm(one, rows[a]) + mm(two, rows[a + 1]) for a in range(0, reps, 2)]
+        picked = [rows.reshape(plane, near, lanes) for rows in picked]
+        s["ysend"][k][h] = jnp.concatenate(picked, axis=1).astype(BF16)
+
+    def plane_sends(source, dest, stage, sem):
         def send(core, move):
             qx = lax.rem(x + move[0], xs) * CORES + lax.rem(c + core, CORES)
             py = lax.rem(y + move[1], reps)
             pltpu.make_async_remote_copy(
                 src_ref=source(qx, py),
-                dst_ref=dest.at[h, half, p],
+                dst_ref=dest.at[p],
                 send_sem=s["send_sem"].at[stage],
-                recv_sem=s["recv_sem"].at[stage, h, half],
+                recv_sem=sem,
                 device_id=(z * PER_Z + qx, py),
                 device_id_type=MESH,
             ).start()
@@ -161,32 +184,35 @@
     others_z = pl.ds(0, zs - 1)
     others_p = pl.ds(0, plane - 1)
 
-    def to_place(h, half):
-        plane_sends(lambda qx, py: s["ysend"].at[h, half, qx * reps + py], s["yrecv"], 0, h, half)
-        s["yrecv"][h, half, p] = s["ysend"][h, half, p]
-
-    def to_owner(h, half):
-        wait_bytes(s["yrecv"].at[h, half, others_p], s["recv_sem"].at[0, h, half])
+    def to_place(h, k):
+        send, recv = s["ysend"][k], s["yrecv"][k]
+        plane_sends(lambda qx, py: send.at[h, qx * reps + py], recv.at[h], 0, s["y_sem"].at[h, k])
+        recv[h, p] = send[h, p]
+
+    def to_owner(h, k):
+        recv, send, size = s["yrecv"][k], s["zsend"][k], sizes[k]
+        wait_bytes(recv.at[h, others_p], s["y_sem"].at[h, k])
         parts = []
-        for k in range(PER_Z):
-            total = s["yrecv"][h, half, k * reps].astype(F32)
+        for at in range(PER_Z):
+            total = recv[h, at * reps].astype(F32)
             for other in range(1, reps):
-                total = total + s["yrecv"][h, half, k * reps + other].astype(F32)
+                total = total + recv[h, at * reps + other].astype(F32)
             parts.append((total * (1.0 / reps)).astype(BF16))
         averaged = jnp.concatenate(parts, axis=0)
-        s["zsend"][h, half] = mm(s["to_z"][...], averaged).astype(BF16).reshape(near, plane, lanes)
-
-        def step(k, carry):
-            r = half * near + k
+        turn = s["to_z"][...] if k == 0 else s["to_z_few"][...]
+        send[h] = mm(turn, averaged).astype(BF16).reshape(size, plane, lanes)
+
+        def step(at, carry):
+            r = sum(sizes[:k]) + at
             odd = lax.rem(r, 2)
             away = near - (r + 1) // 2
             other = lax.rem(z + odd * away + (1 - odd) * (zs - away), zs)
-            z_send(s["zsend"].at[h, half, k], s["zrecv"].at[h, z], 1, s["recv_sem"].at[1, h, 0], other)
+            z_send(send.at[h, at], s["zrecv"].at[h, z], 1, s["recv_sem"].at[1, h, 0], other)
             return carry
 
-        lax.fori_loop(0, near - half, step, 0)
-        if half == 1:
-            s["zrecv"][h, z] = s["zsend"][h, 1, near - 1]
+        lax.fori_loop(0, size - (k == 2), step, 0)
+        if k == 2:
+            s["zrecv"][h, z] = send[h, size - 1]
 
     rows_copy.wait()
     gather(0, 0)
@@ -194,15 +220,22 @@
     to_place(0, 0)
     row, col = iota((part, part), 0), iota((part, part), 1)
     s["to_z"][...] = one_hot(col == ((row & (plane - 1)) << n_bits) + (row >> p_bits))
+    row_few, col_few = iota((part // 2, part // 2), 0), iota((part // 2, part // 2), 1)
+    s["to_z_few"][...] = one_hot(col_few == ((row_few & (plane - 1)) << (n_bits - 1)) + (row_few >> p_bits))
     for h in range(1, groups):
         gather(h, 0)
         to_place(h, 0)
+    fill_near()
     for h in range(groups):
         gather(h, 1)
         to_owner(h, 0)
         to_place(h, 1)
     for h in range(groups):
-        to_owner(h, 1)
+        gather(h, 2)
+        to_place(h, 2)
+    for k in (1, 2):
+        for h in range(groups):
+            to_owner(h, k)
 
     slot_c = jnp.sum(jnp.where(same & (b1 < b0), 1.0, 0.0), axis=1, keepdims=True).astype(jnp.int32)
     of_key = one_hot(iota((nb, keys), 1) == place(owner_c * reps + slot_c))
@@ -259,17 +292,22 @@
         wait_bytes(s["brecv"].at[h, half, pl.ds(0, near - half)], s["recv_sem"].at[2, h, half])
         rows = mm(s["to_place"][...], s["brecv"][h, half].reshape(part, lanes)).astype(BF16)
         s["psend"][h, half] = rows.reshape(PER_Z, reps * near, lanes)
-        plane_sends(lambda qx, py: s["psend"].at[h, half, qx], s["precv"], 3, h, half)
+        plane_sends(lambda qx, py: s["psend"].at[h, half, qx], s["precv"].at[h, half], 3, s["recv_sem"].at[3, h, half])
         s["precv"][h, half, p] = s["psend"][h, half, q]
 
+    def near_rows(h):
+        wait_bytes(s["precv"].at[h, 1, others_p], s["recv_sem"].at[3, h, 1])
+        piece = s["precv"][h, 1].astype(F32)
+        for a in range(reps):
+            at_a = piece[:, a * near : (a + 1) * near].reshape(part, lanes).astype(BF16)
+            s["near"][h, a] = mm(s["to_block"][:, part:], at_a).astype(BF16)
+
     def write(h):
-        pieces = []
-        for half in range(2):
-            wait_bytes(s["precv"].at[h, half, others_p], s["recv_sem"].at[3, h, half])
-            pieces.append(s["precv"][h, half].astype(F32))
+        wait_bytes(s["precv"].at[h, 0, others_p], s["recv_sem"].at[3, h, 0])
+        piece = s["precv"][h, 0].astype(F32)
         for a in range(reps):
-            at_a = [piece[:, a * near : (a + 1) * near].reshape(part, lanes) for piece in pieces]
-            rows = mm(s["to_block"][...], jnp.concatenate(at_a, axis=0).astype(BF16)).astype(BF16)
+            at_a = piece[:, a * near : (a + 1) * near].reshape(part, lanes).astype(BF16)
+            rows = mm(s["to_block"][:, :part], at_a).astype(BF16) + s["near"][h, a]
             for j in range(jb):
                 at = j * extent + h * lanes
                 s["rows"][a, :, at : at + lanes] = rows[j * rb : (j + 1) * rb]
@@ -281,12 +319,13 @@
         back(h, 1)
     for h in range(groups):
         back(h, 0)
+        near_rows(h)
         if h > 0:
             write(h - 1)
     write(groups - 1)
 
     wait_bytes(s["rows"], s["local_sem"].at[3])
-    wait_bytes(s["ysend"].at[:, :, others_p], s["send_sem"].at[0])
+    wait_bytes(s["precv"].at[:, :, others_p], s["send_sem"].at[0])
     wait_bytes(s["zrecv"].at[:, others_z], s["send_sem"].at[1])
     wait_bytes(s["bsend"].at[:, others_z], s["send_sem"].at[2])
     wait_bytes(s["precv"].at[:, :, others_p], s["send_sem"].at[3])
@@ -311,23 +350,29 @@
     by_z = pltpu.VMEM((groups, zs, plane, LANES), BF16)
     by_half = pltpu.VMEM((groups, 2, zs // 2, plane, LANES), BF16)
     by_place = pltpu.VMEM((groups, 2, plane, rows * zs // 2, LANES), BF16)
+    sizes = (zs // 2, zs // 4, zs // 4)
+    by_part = [pltpu.VMEM((groups, plane, rows * size, LANES), BF16) for size in sizes]
     scratch = dict(
         rows=pltpu.VMEM((rows, rb, width), BF16),
         stats=pltpu.VMEM((2, extent, extent), F32),
-        ysend=by_place,
-        yrecv=by_place,
-        zsend=by_half,
+        ysend=by_part,
+        yrecv=by_part,
+        zsend=[pltpu.VMEM((groups, size, plane, LANES), BF16) for size in sizes],
         zrecv=by_z,
         bsend=by_z,
         brecv=by_half,
         psend=pltpu.VMEM((groups, 2, PER_Z, rows * zs // 2, LANES), BF16),
         precv=by_place,
-        to_key=pltpu.VMEM((keys, nb), BF16),
+        near=pltpu.VMEM((groups, rows, nb, LANES), BF16),
+        to_far=pltpu.VMEM((keys // 2, nb), BF16),
+        to_near=pltpu.VMEM((2, 2, keys // 2, nb), BF16),
+        to_z_few=pltpu.VMEM((keys // 4, keys // 4), BF16),
         to_block=pltpu.VMEM((nb, keys), BF16),
         to_place=pltpu.VMEM((keys // 2, keys // 2), BF16),
         to_z=pltpu.VMEM((keys // 2, keys // 2), BF16),
         gmat=pltpu.VMEM((extent, extent), BF16),
         local_sem=dma((4,)),
+        y_sem=dma((groups, 3)),
         send_sem=dma((4,)),
         recv_sem=dma((4, groups, 2)),
     )

time: 92.1 us -> 90.9 us (0.987)
  no operation moved by 1% of the time
where the time goes in v4:
time: 90.9 us; the launch traced here: 90.8 us
  Pallas kernels  88.3 us (97%)
  local copies, waits for them, and re-layouts  2.51 us (3%)
    pallas_call x1, Pallas kernels, per_device(): pl.pallas_call(functools.partial(kernel, (zs, reps, extent, rb, jb, group...  88.3 us
    unnamed x1, local copies, waits for them, and re-layouts  2.51 us

profile of v4, /device:TPU:1, one launch (start us, length us, event | category | flops | bytes accessed | tf_op | source)
XLA Modules:
  0.0 90.8 jit_solution(15643233091137987887)
XLA Ops:
  0.0 88.3 %shard_map.46 = bf16[4,48,3584]{2,1,0:T(8,128)(2,1)} custom-call(s32[336]{0:T(512)} %owner.1, bf16[4,48,3584]{2,1,0:T(8,128)(2,1)} %bitcast.1, f32[1,512,512]{2,1,0:T(8,128)} %left.1, f32[1,512,512]{2,1,0:T(8,128)} %right.1), custom_call_target="tpu_custom_call" | custom-call | tf_op jit(solution)/shard_map/pallas_call | solution.py:379
  88.3 2.5 %copy.6 = bf16[4,48,3584]{2,1,0:T(8,128)(2,1)} copy(bf16[4,48,3584]{2,1,0:T(8,128)(2,1)} %shard_map.46) | data formatting | bytes 2752512
